TPU v7x, 32 devices: a whole 2x2x4 slice. The times are simulated.
32 devices in a mesh: gy: 16 (over z, x, core), gz: 2 (over y).
Axes of the slice: x: 2, y: 2, z: 4, core: 2. Of those that a mesh axis runs over, the one named last changes fastest.
Arguments:
- level_set: float32 [16, 256, 2048], P('gz', 'gy'), may hold values from -6 to 6
- velocity: float32 [3, 16, 256, 2048], P(None, 'gz', 'gy'), may hold values from -6 to 6
Outputs:
- force: float32 [3, 16, 256, 2048], P(None, 'gz', 'gy')
- spectrum: float32 [16, 2, 1024, 256], P('gz', None, 'gy')
All inputs are finite; a program needn't handle non-finite values.
Results may differ from a plain program's by a relative error of at most 0.00007.
Values sent between devices are 32-bit elements; how exact they have to be, the bound alone decides.
A program may use at most 128 MiB of HBM per device.

v0:
```python
import functools
import math

import jax
import jax.numpy as jnp
import ml_dtypes
import numpy as np
from jax import lax
from jax.experimental import pallas as pl
from jax.experimental.pallas import tpu as pltpu
from jax.sharding import PartitionSpec as P

X = 2048


surface_tension = 1.0
time_step = 0.5


def padded_2(cells, sides, width):
    for axis, dim in sides:
        count = lax.axis_size(axis)
        head = lax.slice_in_dim(cells, 0, width, axis=dim)
        tail = lax.slice_in_dim(cells, cells.shape[dim] - width, cells.shape[dim], axis=dim)
        cells = jnp.concatenate(
            [
                lax.ppermute(tail, axis, [(i, (i + 1) % count) for i in range(count)]),
                cells,
                lax.ppermute(head, axis, [((i + 1) % count, i) for i in range(count)]),
            ],
            axis=dim,
        )
    return cells


def slope_depth(field):
    return (field[..., 2:, 1:-1, :] - field[..., :-2, 1:-1, :]) * 0.5


def slope_span(field):
    return (field[..., 1:-1, 2:, :] - field[..., 1:-1, :-2, :]) * 0.5


def slope_line(field):
    inner = field[..., 1:-1, 1:-1, :]
    return (jnp.roll(inner, -1, -1) - jnp.roll(inner, 1, -1)) * 0.5


def normals_from(level):
    grad_x = slope_line(level)
    grad_y = slope_span(level)
    grad_z = slope_depth(level)
    scale = jnp.sqrt(grad_x * grad_x + grad_y * grad_y + grad_z * grad_z + 1.0)
    return jnp.stack([grad_x / scale, grad_y / scale, grad_z / scale])


def divergence(field):
    return slope_line(field[0]) + slope_span(field[1]) + slope_depth(field[2])


def heavy_slopes(level):
    heavy = 0.5 * (1.0 + jnp.tanh(level))
    return jnp.stack([slope_line(heavy), slope_span(heavy), slope_depth(heavy)])


MESH = pl.DeviceIdType.MESH


def halves(table):
    high = table.astype(np.float32).astype(ml_dtypes.bfloat16)
    low = (table - high.astype(np.float64)).astype(np.float32).astype(ml_dtypes.bfloat16)
    return np.stack([high, low])


def line_tables(line, peers):
    position = np.arange(line)[:, None]
    wavenum = np.arange(line // 2)[None, :]
    phase = (position * wavenum % line) * (2.0 * math.pi / line)
    nyquist = np.where(position % 2 == 0, 1.0, -1.0)
    second = np.where(wavenum == 0, nyquist, -np.sin(phase))
    table = np.stack([np.cos(phase), second], axis=1) / math.sqrt(line)
    own = line // 2 // peers
    table = table.reshape(line, 2, peers, own).transpose(2, 0, 1, 3).reshape(peers, line, 2 * own)
    table = table.reshape(peers // 2, 2, line, 2 * own).transpose(0, 2, 1, 3)
    return halves(table.reshape(peers // 2, line, 4 * own))


def span_tables(span):
    index = np.arange(span)
    phase = (index[:, None] * index[None, :] % span) * (2.0 * math.pi / span)
    return halves(np.concatenate([np.cos(phase), np.sin(phase)], axis=1) / math.sqrt(span))


def split(value):
    high = value.astype(jnp.bfloat16)
    return high, (value - high.astype(jnp.float32)).astype(jnp.bfloat16)


def dot3(left, high, low):
    rows = left.shape[0]
    first, rest = split(left)
    both = jnp.dot(jnp.concatenate([first, rest], axis=0), high, preferred_element_type=jnp.float32)
    return both[:rows] + both[rows:] + jnp.dot(first, low, preferred_element_type=jnp.float32)


def rolled(value, step, axis):
    return pltpu.roll(value, (-step) % value.shape[axis], axis)


def rise(value, axis):
    return rolled(value, 1, axis) - rolled(value, -1, axis)


def whole_kernel(
    peers, slabs, level_hbm, vel_hbm, line_hbm, span_hbm, force_ref, out_ref,
    line_tab, span_tab, lev, vel_x, vel_y, vel_z, nor_x, nor_y, nor_z, act, mix_x, mix_y, mix_z,
    lhs, pack, edge, corner_out, corner_in, sent, got,
    load_sem, edge_send, edge_recv, corner_send, corner_recv, deep_send, deep_recv, vz_send, vz_recv, send_sem, recv_sem,
):
    me = lax.axis_index("gy")
    slab = lax.axis_index("gz")
    chips = peers // 2
    chip = me // 2
    core = me % 2
    depth, span, line = level_hbm.shape
    wide = span + 8
    chunks = depth // 2

    def place(dy, dz):
        return {"gy": (me + dy) % peers, "gz": (slab + dz) % slabs}

    loads = [
        pltpu.make_async_copy(level_hbm, lev.at[pl.ds(3, depth), pl.ds(0, span)], load_sem.at[0]),
        pltpu.make_async_copy(vel_hbm.at[1], vel_y.at[:, pl.ds(0, span)], load_sem.at[1]),
        pltpu.make_async_copy(vel_hbm.at[2], vel_z.at[pl.ds(1, depth)], load_sem.at[2]),
        pltpu.make_async_copy(vel_hbm.at[0], vel_x, load_sem.at[3]),
        pltpu.make_async_copy(line_hbm, line_tab, load_sem.at[4]),
        pltpu.make_async_copy(span_hbm, span_tab, load_sem.at[5]),
    ]
    for load in loads:
        load.start()

    greeted = {(off, 0) for off in range(1, peers)}
    greeted |= {(dy % peers, dz % slabs) for dy in (-1, 0, 1) for dz in (-1, 1)}
    barrier = pltpu.get_barrier_semaphore()
    for dy, dz in sorted(greeted):
        pl.semaphore_signal(barrier, inc=1, device_id=place(dy, dz), device_id_type=MESH)
    pl.semaphore_wait(barrier, len(greeted))

    def remote(src, dst, send, recv, target):
        return pltpu.make_async_remote_copy(
            src_ref=src, dst_ref=dst, send_sem=send, recv_sem=recv, device_id=target, device_id_type=MESH)

    deep = {}
    for near in range(1, 4):
        deep[near] = [
            remote(level_hbm.at[near - 1], lev.at[depth + 2 + near, pl.ds(0, span)],
                   deep_send.at[near - 1, 0], deep_recv.at[near - 1, 0], place(0, -1)),
            remote(level_hbm.at[depth - near], lev.at[3 - near, pl.ds(0, span)],
                   deep_send.at[near - 1, 1], deep_recv.at[near - 1, 1], place(0, 1)),
        ]
    deep_vel = [
        remote(vel_hbm.at[2, 0], vel_z.at[depth + 1], vz_send.at[0], vz_recv.at[0], place(0, -1)),
        remote(vel_hbm.at[2, depth - 1], vel_z.at[0], vz_send.at[1], vz_recv.at[1], place(0, 1)),
    ]
    edges = [
        remote(pack.at[side], edge.at[side], edge_send.at[side], edge_recv.at[side], place(2 * side - 1, 0))
        for side in range(2)
    ]
    corners = [
        remote(corner_out.at[i], corner_in.at[i], corner_send.at[i], corner_recv.at[i],
               place(2 * (i % 2) - 1, 2 * (i // 2) - 1))
        for i in range(4)
    ]
    for copy in deep[1]:
        copy.start()
    loads[0].wait()
    loads[1].wait()
    for layer in range(depth):
        pack[0, layer, 0:3] = lev[3 + layer, 0:3]
        pack[0, layer, 3:4] = vel_y[layer, 0:1]
        pack[1, layer, 0:3] = lev[3 + layer, span - 3:span]
        pack[1, layer, 3:4] = vel_y[layer, span - 1:span]
    for copy in edges:
        copy.start()
    for i in range(4):
        first, second = ((3, 4), (depth + 2, depth + 1))[i // 2]
        if i % 2 == 0:
            corner_out[i, 0:2] = lev[first, 0:2]
            corner_out[i, 2:3] = lev[second, 0:1]
        else:
            corner_out[i, 0:2] = lev[first, span - 2:span]
            corner_out[i, 2:3] = lev[second, span - 1:span]
        corner_out[i, 3:4] = jnp.zeros((1, line), jnp.float32)
        corners[i].start()
    for near in (2, 3):
        for copy in deep[near]:
            copy.start()
    for copy in deep_vel:
        copy.start()
    loads[2].wait()
    loads[3].wait()
    for copy in edges:
        copy.wait_recv()
    for layer in range(depth):
        lev[3 + layer, span:span + 3] = edge[0, layer, 0:3]
        vel_y[layer, span:span + 1] = edge[0, layer, 3:4]
        lev[3 + layer, wide - 3:wide] = edge[1, layer, 0:3]
        vel_y[layer, wide - 1:wide] = edge[1, layer, 3:4]

    def normals(p):
        here = lev[p]
        dx = rise(here, 1)
        dy = rise(here, 0)
        dz = lev[p + 1] - lev[p - 1]
        scale = lax.rsqrt(dx * dx + dy * dy + dz * dz + 4.0)
        nor_x[p] = dx * scale
        nor_y[p] = dy * scale
        nor_z[p] = dz * scale
        act[p] = jnp.tanh(here)

    def forces(p, inner):
        bend = -0.125 * (rise(nor_x[p], 1) + rise(nor_y[p], 0) + nor_z[p + 1] - nor_z[p - 1])
        own = bend[:span]
        force_z = own * (act[p + 1, :span] - act[p - 1, :span])
        mix_z[p] = vel_z[p - 2] + time_step * force_z
        if inner:
            here = act[p]
            force_x = own * rise(here[:span], 1)
            force_y = bend * rise(here, 0)
            force_ref[0, p - 3] = force_x
            force_ref[1, p - 3] = force_y[:span]
            force_ref[2, p - 3] = force_z
            mix_x[p - 3] = vel_x[p - 3] + time_step * force_x
            mix_y[p - 3] = vel_y[p - 3] + time_step * force_y

    def source(p):
        return 0.5 * (rise(mix_x[p - 3], 1) + rise(mix_y[p - 3], 0)[:span] + mix_z[p + 1] - mix_z[p - 1])

    def each(first, last, ends_only, body):
        if ends_only:
            pl.loop(0, 2)(lambda i: body(first + i * (last - first)))
        else:
            pl.loop(first, last + 1)(body)

    for chunk in range(chunks):
        low = 2 + chunks - chunk
        high = 3 + chunks + chunk
        near = 6 - low
        if near >= 1:
            for copy in deep[near]:
                copy.wait_recv()
        if near == 1:
            for copy in corners:
                copy.wait_recv()
        if near in (1, 2):
            rows = 2 if near == 1 else 1
            begin = 0 if near == 1 else 2
            for i in range(4):
                layer = depth + 2 + near if i // 2 == 0 else 3 - near
                row = span if i % 2 == 0 else wide - rows
                lev[layer, row:row + rows] = corner_in[i, begin:begin + rows]
        each(low - 2, high + 2, chunk > 0, normals)
        if low == 3:
            for copy in deep_vel:
                copy.wait_recv()
        each(low - 1, high + 1, chunk > 0, functools.partial(forces, inner=low > 3))
        for i, p in enumerate((low, high)):
            first, rest = split(source(p))
            lhs[i * span:(i + 1) * span] = first
            lhs[(2 + i) * span:(3 + i) * span] = rest
        if chunk == 0:
            loads[4].wait()

        def transform(target):
            both = jnp.dot(lhs[...], line_tab[0, target], preferred_element_type=jnp.float32)
            block = both[:2 * span] + both[2 * span:] + jnp.dot(
                lhs[0:2 * span], line_tab[1, target], preferred_element_type=jnp.float32)
            half = block.shape[1] // 2
            return [block[:, side * half:(side + 1) * half].reshape(2, span, half) for side in range(2)]

        @pl.loop(0, chips - 1)
        def _(step):
            target = (chip + chips // 2 + step + step // (chips // 2)) % chips
            blocks = transform(target)
            for side in range(2):
                sent[chunk, step, side] = blocks[side]
                remote(sent.at[chunk, step, side], got.at[chunk, me], send_sem.at[chunk, step, side],
                       recv_sem.at[chunk, me], {"gy": 2 * target + side, "gz": slab}).start()

        blocks = transform(chip)
        for side in range(2):
            sent[chunk, chips - 1, side] = blocks[side]
        remote(sent.at[chunk, chips - 1, 1 - core], got.at[chunk, me], send_sem.at[chunk, chips - 1, 0],
               recv_sem.at[chunk, me], {"gy": 2 * chip + 1 - core, "gz": slab}).start()
        got[chunk, me] = sent[chunk, chips - 1, core]

    loads[5].wait()
    total = peers * span
    for chunk in range(chunks):
        @pl.loop(1, peers)
        def _(off):
            origin = (me + off) % peers
            remote(sent.at[chunk, 0, 0], got.at[chunk, origin], send_sem.at[chunk, 0, 0],
                   recv_sem.at[chunk, origin], {"gy": origin, "gz": slab}).wait_recv()
        for i, layer in enumerate((chunks - 1 - chunk, chunks + chunk)):
            lines = got[chunk, :, i].reshape(total, -1).T
            own = lines.shape[0] // 2
            product = dot3(lines, span_tab[0], span_tab[1])
            out_ref[layer, 0] = product[:own, :total] + product[own:, total:]
            out_ref[layer, 1] = product[own:, :total] - product[:own, total:]
    for copy in deep[1] + deep[2] + deep[3] + deep_vel + edges + corners:
        copy.wait_send()
    for chunk in range(chunks):
        @pl.loop(0, chips - 1)
        def _(step):
            for side in range(2):
                remote(sent.at[chunk, step, side], got.at[chunk, me], send_sem.at[chunk, step, side],
                       recv_sem.at[chunk, me], {"gy": (me + 1) % peers, "gz": slab}).wait_send()
        remote(sent.at[chunk, chips - 1, 0], got.at[chunk, me], send_sem.at[chunk, chips - 1, 0],
               recv_sem.at[chunk, me], {"gy": (me + 1) % peers, "gz": slab}).wait_send()


def whole_by_kernel(level_set, velocity, peers, slabs):
    depth, span, line = level_set.shape
    own = line // 2 // peers
    wide = span + 8
    chunks = depth // 2
    vmem = pl.BlockSpec(memory_space=pltpu.VMEM)
    hbm = pl.BlockSpec(memory_space=pl.ANY)
    f32 = lambda *shape: pltpu.VMEM(shape, jnp.float32)
    dma = lambda *shape: pltpu.SemaphoreType.DMA(shape)
    return pl.pallas_call(
        functools.partial(whole_kernel, peers, slabs),
        out_shape=(
            jax.ShapeDtypeStruct((3, depth, span, line), jnp.float32),
            jax.ShapeDtypeStruct((depth, 2, own, peers * span), jnp.float32),
        ),
        in_specs=[hbm, hbm, hbm, hbm],
        out_specs=(vmem, vmem),
        scratch_shapes=[
            pltpu.VMEM((2, peers // 2, line, 4 * own), jnp.bfloat16),
            pltpu.VMEM((2, peers * span, 2 * peers * span), jnp.bfloat16),
            f32(depth + 6, wide, line),
            f32(depth, span, line),
            f32(depth, wide, line),
            f32(depth + 2, span, line),
            f32(depth + 6, wide, line),
            f32(depth + 6, wide, line),
            f32(depth + 6, wide, line),
            f32(depth + 6, wide, line),
            f32(depth, span, line),
            f32(depth, wide, line),
            f32(depth + 6, span, line),
            pltpu.VMEM((4 * span, line), jnp.bfloat16),
            f32(2, depth, 4, line),
            f32(2, depth, 4, line),
            f32(4, 4, line),
            f32(4, 4, line),
            f32(chunks, peers // 2, 2, 2, span, 2 * own),
            f32(chunks, peers, 2, span, 2 * own),
            dma(6), dma(2), dma(2), dma(4), dma(4), dma(3, 2), dma(3, 2), dma(2), dma(2),
            dma(chunks, peers // 2, 2), dma(chunks, peers),
        ],
        compiler_params=pltpu.CompilerParams(
            collective_id=0, has_side_effects=True, vmem_limit_bytes=58 * 2**20),
    )(level_set, velocity, jnp.asarray(line_tables(line, peers)), jnp.asarray(span_tables(peers * span)))


def on_device(level_set, velocity):
    peers, slabs = lax.axis_size("gy"), lax.axis_size("gz")
    depth, span, line = level_set.shape
    if peers % 4 == 0 and slabs > 1 and line == 128 * peers and span % 16 == 0 and depth % 2 == 0 and depth >= 8:
        return whole_by_kernel(level_set, velocity, peers, slabs)
    padded = padded_2(level_set, (("gy", 1), ("gz", 0)), 3)
    vel_wide = padded_2(velocity, (("gy", 2), ("gz", 1)), 1)
    kappa = -divergence(normals_from(padded))
    force_wide = surface_tension * kappa * heavy_slopes(padded[1:-1, 1:-1])
    force_own = force_wide[:, 1:-1, 1:-1]
    div_force = divergence(force_wide)
    source = divergence(vel_wide) + time_step * div_force
    depth_cells = source.shape[0]
    span_cells = source.shape[1]
    half_len = X // 2
    span_total = span_cells * lax.axis_size("gy")
    position = jnp.arange(X, dtype=jnp.int32)[:, None]
    wavenum = jnp.arange(half_len, dtype=jnp.int32)[None, :]
    phase = (position * wavenum % X).astype(jnp.float32) * (2.0 * math.pi / X)
    nyquist = jnp.where(position % 2 == 0, 1.0, -1.0).astype(jnp.float32)
    second = jnp.where(wavenum == 0, nyquist, -jnp.sin(phase))
    line_table = (jnp.stack([jnp.cos(phase), second], axis=1) / math.sqrt(X)).reshape(X, X)
    transformed = jnp.dot(
        source.reshape(-1, X),
        line_table,
        precision=lax.Precision.HIGHEST,
        preferred_element_type=jnp.float32,
    )
    transformed = transformed.reshape(depth_cells, span_cells, 2, half_len)
    rows_index = jnp.arange(span_total, dtype=jnp.int32)[:, None]
    cols_index = jnp.arange(span_total, dtype=jnp.int32)[None, :]
    span_phase = (rows_index * cols_index % span_total).astype(jnp.float32) * (
        2.0 * math.pi / span_total
    )
    span_cos = jnp.cos(span_phase) / math.sqrt(span_total)
    span_sin = jnp.sin(span_phase) / math.sqrt(span_total)
    piece = lax.all_to_all(transformed, "gy", split_axis=3, concat_axis=1, tiled=True)
    first = piece[:, :, 0, :]
    other = piece[:, :, 1, :]
    high = lax.Precision.HIGHEST
    first_cos = jnp.einsum("nyk,yq->nkq", first, span_cos, precision=high)
    first_sin = jnp.einsum("nyk,yq->nkq", first, span_sin, precision=high)
    other_cos = jnp.einsum("nyk,yq->nkq", other, span_cos, precision=high)
    other_sin = jnp.einsum("nyk,yq->nkq", other, span_sin, precision=high)
    spectrum = jnp.stack([first_cos + other_sin, other_cos - first_sin], axis=1)
    return (force_own, spectrum)


def solution(mesh):
    placed = (P("gz", "gy", None), P(None, "gz", "gy", None))
    return jax.shard_map(
        on_device,
        mesh=mesh,
        in_specs=placed,
        out_specs=(P(None, "gz", "gy", None), P("gz", None, "gy", None)),
        check_vma=False,
    )
```

profile of v0, /device:TPU:0, one launch (start us, length us, event | category | flops | bytes accessed | tf_op | source)
XLA Modules:
  0.0 51.2 jit_solution(6269555317197106778)
XLA Ops:
  0.6 45.6 %shard_map.59 = (f32[3,8,16,2048]{3,2,1,0:T(8,128)}, f32[8,2,64,256]{3,2,1,0:T(8,128)}) custom-call(f32[8,16,2048]{2,1,0:T(8,128)} %level_hbm.1, f32[3,8,16,2048]{3,2,1,0:T(8,128)} %vel_hbm.1, bf16[2,8,2048,256]{3,2,1,0:T(8,128)(2,1)} %constant.4.clone.line_hbm, bf16[2,256,512]{2,1,0:T(8,128)(2,1)} %constant.5.clone.span_hbm), custom_call_target="tpu_custom_call" | custom-call | tf_op jit(solution)/shard_map/pallas_call | solution.py:333
  46.2 0.0 copy-start
  46.2 4.0 %copy.8 = f32[3,8,16,2048]{3,2,1,0:T(8,128)} copy(f32[3,8,16,2048]{3,2,1,0:T(8,128)} %get-tuple-element.4) | data formatting | bytes 6291456
  50.2 0.0 copy-done
  50.2 1.0 %copy.9 = f32[8,2,64,256]{3,2,1,0:T(8,128)} copy(f32[8,2,64,256]{3,2,1,0:T(8,128)S(1)} %copy-done) | data formatting | bytes 2097152
Async XLA Ops:
  46.2 4.0 %copy-start = (f32[8,2,64,256]{3,2,1,0:T(8,128)S(1)}, f32[8,2,64,256]{3,2,1,0:T(8,128)}, u32[]{:S(2)}) copy-start(f32[8,2,64,256]{3,2,1,0:T(8,128)} %get-tuple-element.5) | copy-start | bytes 3145732
where the time goes:
time: 51.4 us; the launch traced here: 51.2 us
  Pallas kernels  45.6 us (89%)
  local copies, waits for them, and re-layouts  4.97 us (10%)
  between operations  0.65 us (1%)
    pallas_call x1, Pallas kernels, whole_by_kernel(): pl.pallas_call(functools.partial(whole_kernel, peers, slabs), out_shape=(...  45.6 us
    unnamed x4, local copies, waits for them, and re-layouts  4.97 us

commit v1 on v0

--- a/solution.py
+++ b/solution.py
@@ -73,16 +73,15 @@
 
 
 def line_tables(line, peers):
-    position = np.arange(line)[:, None]
+    position = np.arange(line // 2)[:, None]
     wavenum = np.arange(line // 2)[None, :]
     phase = (position * wavenum % line) * (2.0 * math.pi / line)
     nyquist = np.where(position % 2 == 0, 1.0, -1.0)
     second = np.where(wavenum == 0, nyquist, -np.sin(phase))
     table = np.stack([np.cos(phase), second], axis=1) / math.sqrt(line)
     own = line // 2 // peers
-    table = table.reshape(line, 2, peers, own).transpose(2, 0, 1, 3).reshape(peers, line, 2 * own)
-    table = table.reshape(peers // 2, 2, line, 2 * own).transpose(0, 2, 1, 3)
-    return halves(table.reshape(peers // 2, line, 4 * own))
+    table = table.reshape(line // 2, 2, peers // 4, 4, own // 2, 2).transpose(2, 5, 0, 3, 1, 4)
+    return halves(table.reshape(peers // 4, 2, line // 2, 4 * own))
 
 
 def span_tables(span):
@@ -114,14 +113,14 @@
 def whole_kernel(
     peers, slabs, level_hbm, vel_hbm, line_hbm, span_hbm, force_ref, out_ref,
     line_tab, span_tab, lev, vel_x, vel_y, vel_z, nor_x, nor_y, nor_z, act, mix_x, mix_y, mix_z,
-    lhs, pack, edge, corner_out, corner_in, sent, got,
+    lhs, pack, edge, corner_out, corner_in, sent, got, interim,
     load_sem, edge_send, edge_recv, corner_send, corner_recv, deep_send, deep_recv, vz_send, vz_recv, send_sem, recv_sem,
 ):
     me = lax.axis_index("gy")
     slab = lax.axis_index("gz")
-    chips = peers // 2
-    chip = me // 2
-    core = me % 2
+    fours = peers // 4
+    four = me // 4
+    mine = me % 4
     depth, span, line = level_hbm.shape
     wide = span + 8
     chunks = depth // 2
@@ -266,34 +265,49 @@
                 copy.wait_recv()
         each(low - 1, high + 1, chunk > 0, functools.partial(forces, inner=low > 3))
         for i, p in enumerate((low, high)):
-            first, rest = split(source(p))
-            lhs[i * span:(i + 1) * span] = first
-            lhs[(2 + i) * span:(3 + i) * span] = rest
+            cells = source(p)
+            for parity in range(2):
+                near_half, far_half = cells[:, :line // 2], cells[:, line // 2:]
+                first, rest = split(near_half - far_half if parity else near_half + far_half)
+                lhs[parity, i * span:(i + 1) * span] = first
+                lhs[parity, (2 + i) * span:(3 + i) * span] = rest
         if chunk == 0:
             loads[4].wait()
 
         def transform(target):
-            both = jnp.dot(lhs[...], line_tab[0, target], preferred_element_type=jnp.float32)
-            block = both[:2 * span] + both[2 * span:] + jnp.dot(
-                lhs[0:2 * span], line_tab[1, target], preferred_element_type=jnp.float32)
-            half = block.shape[1] // 2
-            return [block[:, side * half:(side + 1) * half].reshape(2, span, half) for side in range(2)]
-
-        @pl.loop(0, chips - 1)
+            pair = []
+            for parity in range(2):
+                both = jnp.dot(lhs[parity], line_tab[0, target, parity], preferred_element_type=jnp.float32)
+                pair.append(both[:2 * span] + both[2 * span:] + jnp.dot(
+                    lhs[parity, 0:2 * span], line_tab[1, target, parity], preferred_element_type=jnp.float32))
+            width = pair[0].shape[1] // 2
+            in_front = lax.broadcasted_iota(jnp.int32, (2 * span, width), 1) < width // 2
+            blocks = []
+            for part in range(2):
+                even, odd = (value[:, part * width:(part + 1) * width] for value in pair)
+                blocks.append(jnp.where(in_front, even, pltpu.roll(odd, width // 2, 1)))
+                blocks.append(jnp.where(in_front, pltpu.roll(even, width // 2, 1), odd))
+            return [block.reshape(2, span, width) for block in blocks]
+
+        def send(step, slot, target):
+            return remote(sent.at[chunk, step, slot], got.at[chunk, me], send_sem.at[chunk, step, slot],
+                          recv_sem.at[chunk, me], {"gy": target, "gz": slab})
+
+        @pl.loop(0, fours - 1)
         def _(step):
-            target = (chip + chips // 2 + step + step // (chips // 2)) % chips
+            target = (four + fours // 2 + step + step // (fours // 2)) % fours
             blocks = transform(target)
-            for side in range(2):
-                sent[chunk, step, side] = blocks[side]
-                remote(sent.at[chunk, step, side], got.at[chunk, me], send_sem.at[chunk, step, side],
-                       recv_sem.at[chunk, me], {"gy": 2 * target + side, "gz": slab}).start()
-
-        blocks = transform(chip)
-        for side in range(2):
-            sent[chunk, chips - 1, side] = blocks[side]
-        remote(sent.at[chunk, chips - 1, 1 - core], got.at[chunk, me], send_sem.at[chunk, chips - 1, 0],
-               recv_sem.at[chunk, me], {"gy": 2 * chip + 1 - core, "gz": slab}).start()
-        got[chunk, me] = sent[chunk, chips - 1, core]
+            for slot in range(4):
+                sent[chunk, step, slot] = blocks[slot]
+                send(step, slot, 4 * target + slot).start()
+
+        blocks = transform(four)
+        for slot in range(4):
+            sent[chunk, fours - 1, slot] = blocks[slot]
+        for off in range(1, 4):
+            slot = (mine + off) % 4
+            send(fours - 1, slot, 4 * four + slot).start()
+        got[chunk, me] = sent[chunk, fours - 1, mine]
 
     loads[5].wait()
     total = peers * span
@@ -305,20 +319,69 @@
                    recv_sem.at[chunk, origin], {"gy": origin, "gz": slab}).wait_recv()
         for i, layer in enumerate((chunks - 1 - chunk, chunks + chunk)):
             lines = got[chunk, :, i].reshape(total, -1).T
-            own = lines.shape[0] // 2
+            own = lines.shape[0] // 4
             product = dot3(lines, span_tab[0], span_tab[1])
-            out_ref[layer, 0] = product[:own, :total] + product[own:, total:]
-            out_ref[layer, 1] = product[own:, :total] - product[:own, total:]
+            for parity in range(2):
+                real = product[2 * own * parity:2 * own * parity + own]
+                imag = product[2 * own * parity + own:2 * own * (parity + 1)]
+                rows = pl.ds(parity, own, stride=2)
+                for lane in range(0, total, 128):
+                    turn = slice(total + lane, total + lane + 128)
+                    cols = slice(lane, lane + 128)
+                    interim[0, lane // 128, rows] = real[:, cols] + imag[:, turn]
+                    interim[1, lane // 128, rows] = imag[:, cols] - real[:, turn]
+            for part in range(2):
+                for lane in range(0, total, 128):
+                    out_ref[layer, part, :, lane:lane + 128] = interim[part, lane // 128]
     for copy in deep[1] + deep[2] + deep[3] + deep_vel + edges + corners:
         copy.wait_send()
     for chunk in range(chunks):
-        @pl.loop(0, chips - 1)
+        @pl.loop(0, fours - 1)
         def _(step):
-            for side in range(2):
-                remote(sent.at[chunk, step, side], got.at[chunk, me], send_sem.at[chunk, step, side],
+            for slot in range(4):
+                remote(sent.at[chunk, step, slot], got.at[chunk, me], send_sem.at[chunk, step, slot],
                        recv_sem.at[chunk, me], {"gy": (me + 1) % peers, "gz": slab}).wait_send()
-        remote(sent.at[chunk, chips - 1, 0], got.at[chunk, me], send_sem.at[chunk, chips - 1, 0],
-               recv_sem.at[chunk, me], {"gy": (me + 1) % peers, "gz": slab}).wait_send()
+        for off in range(1, 4):
+            slot = (mine + off) % 4
+            remote(sent.at[chunk, fours - 1, slot], got.at[chunk, me], send_sem.at[chunk, fours - 1, slot],
+                   recv_sem.at[chunk, me], {"gy": (me + 1) % peers, "gz": slab}).wait_send()
+
+
+def settle_kernel(force_in, spec_in, force_out, spec_out, force_mem, spec_mem, in_sem, out_sem):
+    ways = []
+    for part in range(force_in.shape[0]):
+        for piece in range(2):
+            size = force_in.shape[1] // 2
+            ways.append((force_in, force_mem, force_out, (part, pl.ds(piece * size, size))))
+    for piece in range(2):
+        size = spec_in.shape[0] // 2
+        ways.append((spec_in, spec_mem, spec_out, (pl.ds(piece * size, size),)))
+    ins = [pltpu.make_async_copy(a.at[at], b.at[at], in_sem.at[i]) for i, (a, b, c, at) in enumerate(ways)]
+    outs = [pltpu.make_async_copy(b.at[at], c.at[at], out_sem.at[i]) for i, (a, b, c, at) in enumerate(ways)]
+    for copy in ins:
+        copy.start()
+    for first, then in zip(ins, outs):
+        first.wait()
+        then.start()
+    for copy in outs:
+        copy.wait()
+
+
+def settle(force, spec):
+    hbm = pl.BlockSpec(memory_space=pl.ANY)
+    return pl.pallas_call(
+        settle_kernel,
+        out_shape=(jax.ShapeDtypeStruct(force.shape, force.dtype), jax.ShapeDtypeStruct(spec.shape, spec.dtype)),
+        in_specs=[hbm, hbm],
+        out_specs=(hbm, hbm),
+        scratch_shapes=[
+            pltpu.VMEM(force.shape, force.dtype),
+            pltpu.VMEM(spec.shape, spec.dtype),
+            pltpu.SemaphoreType.DMA((8,)),
+            pltpu.SemaphoreType.DMA((8,)),
+        ],
+        compiler_params=pltpu.CompilerParams(vmem_limit_bytes=56 * 2**20),
+    )(force, spec)
 
 
 def whole_by_kernel(level_set, velocity, peers, slabs):
@@ -339,7 +402,7 @@
         in_specs=[hbm, hbm, hbm, hbm],
         out_specs=(vmem, vmem),
         scratch_shapes=[
-            pltpu.VMEM((2, peers // 2, line, 4 * own), jnp.bfloat16),
+            pltpu.VMEM((2, peers // 4, 2, line // 2, 4 * own), jnp.bfloat16),
             pltpu.VMEM((2, peers * span, 2 * peers * span), jnp.bfloat16),
             f32(depth + 6, wide, line),
             f32(depth, span, line),
@@ -352,15 +415,16 @@
             f32(depth, span, line),
             f32(depth, wide, line),
             f32(depth + 6, span, line),
-            pltpu.VMEM((4 * span, line), jnp.bfloat16),
+            pltpu.VMEM((2, 4 * span, line // 2), jnp.bfloat16),
             f32(2, depth, 4, line),
             f32(2, depth, 4, line),
             f32(4, 4, line),
             f32(4, 4, line),
-            f32(chunks, peers // 2, 2, 2, span, 2 * own),
+            f32(chunks, peers // 4, 4, 2, span, 2 * own),
             f32(chunks, peers, 2, span, 2 * own),
+            f32(2, peers * span // 128, own, 128),
             dma(6), dma(2), dma(2), dma(4), dma(4), dma(3, 2), dma(3, 2), dma(2), dma(2),
-            dma(chunks, peers // 2, 2), dma(chunks, peers),
+            dma(chunks, peers // 4, 4), dma(chunks, peers),
         ],
         compiler_params=pltpu.CompilerParams(
             collective_id=0, has_side_effects=True, vmem_limit_bytes=58 * 2**20),
@@ -370,8 +434,8 @@
 def on_device(level_set, velocity):
     peers, slabs = lax.axis_size("gy"), lax.axis_size("gz")
     depth, span, line = level_set.shape
-    if peers % 4 == 0 and slabs > 1 and line == 128 * peers and span % 16 == 0 and depth % 2 == 0 and depth >= 8:
-        return whole_by_kernel(level_set, velocity, peers, slabs)
+    if peers % 8 == 0 and slabs > 1 and line == 128 * peers and span % 16 == 0 and depth % 2 == 0 and depth >= 8:
+        return settle(*whole_by_kernel(level_set, velocity, peers, slabs))
     padded = padded_2(level_set, (("gy", 1), ("gz", 0)), 3)
     vel_wide = padded_2(velocity, (("gy", 2), ("gz", 1)), 1)
     kappa = -divergence(normals_from(padded))

time: 51.4 us -> 48.4 us (0.942)
  local copies, waits for them, and re-layouts: 4.97 us -> 0 us
  Pallas kernels: 45.6 us -> 47.6 us
    unnamed x4 -> x0, local copies, waits for them, and re-layouts: 4.97 us -> none
    pallas_call x0 -> x1, Pallas kernels: none -> 3.58 us  [settle(): pl.pallas_call(settle_kernel, out_shape=(jax.ShapeDtypeStruct(force.shape...]
    pallas_call x1, Pallas kernels: 45.6 us -> 44 us  [whole_by_kernel(): pl.pallas_call(functools.partial(whole_kernel, peers, slabs), out_shape=(...]
where the time goes in v1:
time: 48.4 us; the launch traced here: 48.3 us
  Pallas kernels  47.6 us (98%)
  between operations  0.64 us (1%)
    pallas_call x1, Pallas kernels, whole_by_kernel(): pl.pallas_call(functools.partial(whole_kernel, peers, slabs), out_shape=(...  44 us
    pallas_call x1, Pallas kernels, settle(): pl.pallas_call(settle_kernel, out_shape=(jax.ShapeDtypeStruct(force.shape...  3.58 us

profile of v1, /device:TPU:0, one launch (start us, length us, event | category | flops | bytes accessed | tf_op | source)
XLA Modules:
  0.0 48.3 jit_solution(16533220469587886219)
XLA Ops:
  0.6 44.0 %shard_map.59 = (f32[3,8,16,2048]{3,2,1,0:T(8,128)}, f32[8,2,64,256]{3,2,1,0:T(8,128)}) custom-call(f32[8,16,2048]{2,1,0:T(8,128)} %level_hbm.1, f32[3,8,16,2048]{3,2,1,0:T(8,128)} %vel_hbm.1, bf16[2,4,2,1024,256]{4,3,2,1,0:T(8,128)(2,1)} %constant.4.clone.line_hbm, bf16[2,256,512]{2,1,0:T(8,128)(2,1)} %constant.5.clone.span_hbm), custom_call_target="tpu_custom_call" | custom-call | tf_op jit(solution)/shard_map/pallas_call | solution.py:396
  44.7 3.6 %shard_map.60 = (f32[3,8,16,2048]{3,2,1,0:T(8,128)}, f32[8,2,64,256]{3,2,1,0:T(8,128)}) custom-call(f32[3,8,16,2048]{3,2,1,0:T(8,128)} %get-tuple-element.4.force_in, f32[8,2,64,256]{3,2,1,0:T(8,128)} %get-tuple-element.5.spec_in), custom_call_target="tpu_custom_call" | custom-call | tf_op jit(solution)/shard_map/pallas_call | solution.py:372

commit v2 on v1

--- a/solution.py
+++ b/solution.py
@@ -114,7 +114,7 @@
     peers, slabs, level_hbm, vel_hbm, line_hbm, span_hbm, force_ref, out_ref,
     line_tab, span_tab, lev, vel_x, vel_y, vel_z, nor_x, nor_y, nor_z, act, mix_x, mix_y, mix_z,
     lhs, pack, edge, corner_out, corner_in, sent, got, interim,
-    load_sem, edge_send, edge_recv, corner_send, corner_recv, deep_send, deep_recv, vz_send, vz_recv, send_sem, recv_sem,
+    load_sem, edge_send, edge_recv, corner_send, corner_recv, deep_send, deep_recv, mix_send, mix_recv, send_sem, recv_sem,
 ):
     me = lax.axis_index("gy")
     slab = lax.axis_index("gz")
@@ -131,7 +131,7 @@
     loads = [
         pltpu.make_async_copy(level_hbm, lev.at[pl.ds(3, depth), pl.ds(0, span)], load_sem.at[0]),
         pltpu.make_async_copy(vel_hbm.at[1], vel_y.at[:, pl.ds(0, span)], load_sem.at[1]),
-        pltpu.make_async_copy(vel_hbm.at[2], vel_z.at[pl.ds(1, depth)], load_sem.at[2]),
+        pltpu.make_async_copy(vel_hbm.at[2], vel_z, load_sem.at[2]),
         pltpu.make_async_copy(vel_hbm.at[0], vel_x, load_sem.at[3]),
         pltpu.make_async_copy(line_hbm, line_tab, load_sem.at[4]),
         pltpu.make_async_copy(span_hbm, span_tab, load_sem.at[5]),
@@ -151,16 +151,16 @@
             src_ref=src, dst_ref=dst, send_sem=send, recv_sem=recv, device_id=target, device_id_type=MESH)
 
     deep = {}
-    for near in range(1, 4):
+    for near in range(1, 3):
         deep[near] = [
             remote(level_hbm.at[near - 1], lev.at[depth + 2 + near, pl.ds(0, span)],
                    deep_send.at[near - 1, 0], deep_recv.at[near - 1, 0], place(0, -1)),
             remote(level_hbm.at[depth - near], lev.at[3 - near, pl.ds(0, span)],
                    deep_send.at[near - 1, 1], deep_recv.at[near - 1, 1], place(0, 1)),
         ]
-    deep_vel = [
-        remote(vel_hbm.at[2, 0], vel_z.at[depth + 1], vz_send.at[0], vz_recv.at[0], place(0, -1)),
-        remote(vel_hbm.at[2, depth - 1], vel_z.at[0], vz_send.at[1], vz_recv.at[1], place(0, 1)),
+    deep_mix = [
+        remote(mix_z.at[3], mix_z.at[depth + 3], mix_send.at[0], mix_recv.at[0], place(0, -1)),
+        remote(mix_z.at[depth + 2], mix_z.at[2], mix_send.at[1], mix_recv.at[1], place(0, 1)),
     ]
     edges = [
         remote(pack.at[side], edge.at[side], edge_send.at[side], edge_recv.at[side], place(2 * side - 1, 0))
@@ -192,10 +192,7 @@
             corner_out[i, 2:3] = lev[second, span - 1:span]
         corner_out[i, 3:4] = jnp.zeros((1, line), jnp.float32)
         corners[i].start()
-    for near in (2, 3):
-        for copy in deep[near]:
-            copy.start()
-    for copy in deep_vel:
+    for copy in deep[2]:
         copy.start()
     loads[2].wait()
     loads[3].wait()
@@ -218,20 +215,19 @@
         nor_z[p] = dz * scale
         act[p] = jnp.tanh(here)
 
-    def forces(p, inner):
+    def forces(p):
         bend = -0.125 * (rise(nor_x[p], 1) + rise(nor_y[p], 0) + nor_z[p + 1] - nor_z[p - 1])
         own = bend[:span]
         force_z = own * (act[p + 1, :span] - act[p - 1, :span])
-        mix_z[p] = vel_z[p - 2] + time_step * force_z
-        if inner:
-            here = act[p]
-            force_x = own * rise(here[:span], 1)
-            force_y = bend * rise(here, 0)
-            force_ref[0, p - 3] = force_x
-            force_ref[1, p - 3] = force_y[:span]
-            force_ref[2, p - 3] = force_z
-            mix_x[p - 3] = vel_x[p - 3] + time_step * force_x
-            mix_y[p - 3] = vel_y[p - 3] + time_step * force_y
+        here = act[p]
+        force_x = own * rise(here[:span], 1)
+        force_y = bend * rise(here, 0)
+        force_ref[0, p - 3] = force_x
+        force_ref[1, p - 3] = force_y[:span]
+        force_ref[2, p - 3] = force_z
+        mix_x[p - 3] = vel_x[p - 3] + time_step * force_x
+        mix_y[p - 3] = vel_y[p - 3] + time_step * force_y
+        mix_z[p] = vel_z[p - 3] + time_step * force_z
 
     def source(p):
         return 0.5 * (rise(mix_x[p - 3], 1) + rise(mix_y[p - 3], 0)[:span] + mix_z[p + 1] - mix_z[p - 1])
@@ -246,7 +242,7 @@
         low = 2 + chunks - chunk
         high = 3 + chunks + chunk
         near = 6 - low
-        if near >= 1:
+        if near in (1, 2):
             for copy in deep[near]:
                 copy.wait_recv()
         if near == 1:
@@ -259,11 +255,15 @@
                 layer = depth + 2 + near if i // 2 == 0 else 3 - near
                 row = span if i % 2 == 0 else wide - rows
                 lev[layer, row:row + rows] = corner_in[i, begin:begin + rows]
-        each(low - 2, high + 2, chunk > 0, normals)
+        if low > 3:
+            each(low - 2, high + 2, chunk > 0, normals)
+            each(low - 1, high + 1, chunk > 0, forces)
+        if low == 4:
+            for copy in deep_mix:
+                copy.start()
         if low == 3:
-            for copy in deep_vel:
+            for copy in deep_mix:
                 copy.wait_recv()
-        each(low - 1, high + 1, chunk > 0, functools.partial(forces, inner=low > 3))
         for i, p in enumerate((low, high)):
             cells = source(p)
             for parity in range(2):
@@ -333,7 +333,7 @@
             for part in range(2):
                 for lane in range(0, total, 128):
                     out_ref[layer, part, :, lane:lane + 128] = interim[part, lane // 128]
-    for copy in deep[1] + deep[2] + deep[3] + deep_vel + edges + corners:
+    for copy in deep[1] + deep[2] + deep_mix + edges + corners:
         copy.wait_send()
     for chunk in range(chunks):
         @pl.loop(0, fours - 1)
@@ -407,7 +407,7 @@
             f32(depth + 6, wide, line),
             f32(depth, span, line),
             f32(depth, wide, line),
-            f32(depth + 2, span, line),
+            f32(depth, span, line),
             f32(depth + 6, wide, line),
             f32(depth + 6, wide, line),
             f32(depth + 6, wide, line),
@@ -423,7 +423,7 @@
             f32(chunks, peers // 4, 4, 2, span, 2 * own),
             f32(chunks, peers, 2, span, 2 * own),
             f32(2, peers * span // 128, own, 128),
-            dma(6), dma(2), dma(2), dma(4), dma(4), dma(3, 2), dma(3, 2), dma(2), dma(2),
+            dma(6), dma(2), dma(2), dma(4), dma(4), dma(2, 2), dma(2, 2), dma(2), dma(2),
             dma(chunks, peers // 4, 4), dma(chunks, peers),
         ],
         compiler_params=pltpu.CompilerParams(

time: 48.4 us -> 47.8 us (0.988)
  Pallas kernels: 47.6 us -> 47 us
    pallas_call x1, Pallas kernels: 44 us -> 43.4 us  [whole_by_kernel(): pl.pallas_call(functools.partial(whole_kernel, peers, slabs), out_shape=(...]
where the time goes in v2:
time: 47.8 us; the launch traced here: 47.7 us
  Pallas kernels  47 us (98%)
  between operations  0.64 us (1%)
    pallas_call x1, Pallas kernels, whole_by_kernel(): pl.pallas_call(functools.partial(whole_kernel, peers, slabs), out_shape=(...  43.4 us
    pallas_call x1, Pallas kernels, settle(): pl.pallas_call(settle_kernel, out_shape=(jax.ShapeDtypeStruct(force.shape...  3.58 us

profile of v2, /device:TPU:0, one launch (start us, length us, event | category | flops | bytes accessed | tf_op | source)
XLA Modules:
  0.0 47.7 jit_solution(11152402640747501850)
XLA Ops:
  0.6 43.4 %shard_map.59 = (f32[3,8,16,2048]{3,2,1,0:T(8,128)}, f32[8,2,64,256]{3,2,1,0:T(8,128)}) custom-call(f32[8,16,2048]{2,1,0:T(8,128)} %level_hbm.1, f32[3,8,16,2048]{3,2,1,0:T(8,128)} %vel_hbm.1, bf16[2,4,2,1024,256]{4,3,2,1,0:T(8,128)(2,1)} %constant.4.clone.line_hbm, bf16[2,256,512]{2,1,0:T(8,128)(2,1)} %constant.5.clone.span_hbm), custom_call_target="tpu_custom_call" | custom-call | tf_op jit(solution)/shard_map/pallas_call | solution.py:396
  44.1 3.6 %shard_map.60 = (f32[3,8,16,2048]{3,2,1,0:T(8,128)}, f32[8,2,64,256]{3,2,1,0:T(8,128)}) custom-call(f32[3,8,16,2048]{3,2,1,0:T(8,128)} %get-tuple-element.4.force_in, f32[8,2,64,256]{3,2,1,0:T(8,128)} %get-tuple-element.5.spec_in), custom_call_target="tpu_custom_call" | custom-call | tf_op jit(solution)/shard_map/pallas_call | solution.py:372
